TPU v7x, 32 devices: a whole 2x2x4 slice. The times are simulated.
32 devices in a mesh: grp: 2 (over y), blk: 4 (over x, core), hid: 4 (over z).
Axes of the slice: x: 2, y: 2, z: 4, core: 2. Of those that a mesh axis runs over, the one named last changes fastest.
Arguments:
- tokens: bfloat16 [1024, 4096], P(('grp', 'blk'), 'hid'), parts along dimension 0, may hold values from -6 to 6
- grad_out: bfloat16 [1024, 4096], P(('grp', 'blk'), 'hid'), parts along dimension 0, may hold values from -0.59765625 to 0.59765625
- expert_ids: int32 [1024, 8], P(('grp', 'blk')), parts along dimension 0, may hold values from 0 to 15, all different within a row; in each aligned block of 128 rows (0 to 127, 128 to 255, ...) at most 68 rows name the same one
- route_probs: float32 [1024, 8], P(('grp', 'blk')), parts along dimension 0, may hold values from 0.1 to 1
- gate_w: bfloat16 [16, 4096, 1536], P('blk', None, 'hid'), may hold values from -0.09375 to 0.09375
- up_w: bfloat16 [16, 4096, 1536], P('blk', None, 'hid'), may hold values from -0.09375 to 0.09375
- down_w: bfloat16 [16, 1536, 4096], P('blk', 'hid'), may hold values from -0.15625 to 0.15625
Outputs:
- grad_tokens: bfloat16 [1024, 4096], P(('grp', 'blk'), 'hid'), parts along dimension 0
- grad_gate: bfloat16 [32, 4096, 1536], P(('grp', 'blk'), None, 'hid'), parts along dimension 0
- grad_up: bfloat16 [32, 4096, 1536], P(('grp', 'blk'), None, 'hid'), parts along dimension 0
- grad_down: bfloat16 [32, 1536, 4096], P(('grp', 'blk'), 'hid'), parts along dimension 0
There are 2 independent parts, one for each index of `grp`. A program takes and returns all parts, laid end to end along the dimension named above; an argument that names none is the same for every part. Nothing has to cross between parts.
Inputs may be any that keep to these rules, and one draw needn't show every extreme that they name: `expert_ids`: in the rows of one token group (128 tokens, aligned blocks) each token names 8 different experts, and no expert is named by more than 68 tokens of the group; some expert is named by exactly 68.
All inputs are finite; a program needn't handle non-finite values.
Results may differ from a plain program's by a relative error of at most 0.012.
Values may be sent and summed in bfloat16 or wider, within the bound.
A program may use at most 256 MiB of HBM per device.

v0:
```python
import jax
import jax.numpy as jnp
from jax import lax
from jax.sharding import PartitionSpec as P

TOP = 8
EXPERTS = 16
CAP = 68


def route_tables(routed, weights):
    flat_ids = routed.reshape(-1)
    onehot = (flat_ids[:, None] == jnp.arange(EXPERTS, dtype=jnp.int32)[None, :]).astype(jnp.int32)
    earlier = jnp.cumsum(onehot, axis=0) - onehot
    slot_index = jnp.sum(earlier * onehot, axis=1)
    target = flat_ids * CAP + slot_index
    cells = jnp.arange(EXPERTS * CAP, dtype=jnp.int32)
    match = cells[:, None] == target[None, :]
    owner = jnp.arange(flat_ids.shape[0], dtype=jnp.int32) // TOP
    filled = jnp.any(match, axis=1)
    token_of = jnp.sum(jnp.where(match, owner[None, :], 0), axis=1)
    weight_of = jnp.sum(jnp.where(match, weights.reshape(-1)[None, :], 0.0), axis=1)
    return (target, token_of, weight_of, filled)


def place_rows(features, grads, token_of, weight_of, filled):
    width = features.shape[1]
    slot_x = jnp.where(filled[:, None], jnp.take(features, token_of, axis=0), 0)
    scaled = weight_of[:, None] * jnp.take(grads, token_of, axis=0).astype(jnp.float32)
    slot_g = jnp.where(filled[:, None], scaled, 0.0).astype(jnp.bfloat16)
    return (slot_x.reshape(EXPERTS, CAP, width), slot_g.reshape(EXPERTS, CAP, width))


def per_device(tokens, grad_out, expert_ids, route_probs, gate_w, up_w, down_w):
    local_tokens = tokens.shape[0]
    hidden_part = gate_w.shape[2]
    target, token_of, weight_of, filled = route_tables(expert_ids, route_probs)
    whole_x, whole_g = (
        lax.all_gather(tokens, "hid", axis=1, tiled=True),
        lax.all_gather(grad_out, "hid", axis=1, tiled=True),
    )
    send_x, send_g = place_rows(whole_x, whole_g, token_of, weight_of, filled)
    recv_x, recv_g = (
        lax.all_to_all(send_x, "blk", split_axis=0, concat_axis=1, tiled=True),
        lax.all_to_all(send_g, "blk", split_axis=0, concat_axis=1, tiled=True),
    )
    both_weights = jnp.concatenate((gate_w, up_w), axis=2)
    both_values = jnp.einsum(
        "erd,edf->erf", recv_x, both_weights, preferred_element_type=jnp.float32
    )
    gate_value = both_values[:, :, :hidden_part]
    up_value = both_values[:, :, hidden_part:]
    sigmoid_gate = jax.nn.sigmoid(gate_value)
    activated = gate_value * sigmoid_gate
    hidden = (activated * up_value).astype(jnp.bfloat16)
    grad_down = jnp.einsum(
        "erf,erd->efd", hidden, recv_g, preferred_element_type=jnp.float32
    ).astype(jnp.bfloat16)
    d_hidden = jnp.einsum("erd,efd->erf", recv_g, down_w, preferred_element_type=jnp.float32)
    d_gate_h = (
        d_hidden * up_value * sigmoid_gate * (1.0 + gate_value * (1.0 - sigmoid_gate))
    ).astype(jnp.bfloat16)
    d_up_h = (d_hidden * activated).astype(jnp.bfloat16)
    both_grads = jnp.concatenate((d_gate_h, d_up_h), axis=2)
    weight_grads = jnp.einsum(
        "erd,erf->edf", recv_x, both_grads, preferred_element_type=jnp.float32
    ).astype(jnp.bfloat16)
    grad_gate = weight_grads[:, :, :hidden_part]
    grad_up = weight_grads[:, :, hidden_part:]
    summed = lax.psum_scatter(
        jnp.einsum(
            "edf,erf->der", both_weights, both_grads, preferred_element_type=jnp.float32
        ).astype(jnp.bfloat16),
        "hid",
        scatter_dimension=0,
        tiled=True,
    ).astype(jnp.float32)
    shared = jnp.transpose(summed, (1, 2, 0)).astype(jnp.bfloat16)
    returned = lax.all_to_all(shared, "blk", split_axis=1, concat_axis=0, tiled=True)
    flat_back = returned.reshape(EXPERTS * CAP, returned.shape[2]).astype(jnp.float32)
    picked = jnp.take(flat_back, target, axis=0).reshape(local_tokens, TOP, returned.shape[2])
    grad_tokens = jnp.sum(picked, axis=1).astype(jnp.bfloat16)
    return (grad_tokens, grad_gate, grad_up, grad_down)


def solution(mesh):
    placed = (
        P(("grp", "blk"), "hid"),
        P(("grp", "blk"), "hid"),
        P(("grp", "blk"), None),
        P(("grp", "blk"), None),
        P("blk", None, "hid"),
        P("blk", None, "hid"),
        P("blk", "hid", None),
    )
    return jax.shard_map(
        per_device,
        mesh=mesh,
        in_specs=placed,
        out_specs=(
            P(("grp", "blk"), "hid"),
            P(("grp", "blk"), None, "hid"),
            P(("grp", "blk"), None, "hid"),
            P(("grp", "blk"), "hid", None),
        ),
        check_vma=False,
    )
```

profile of v0, /device:TPU:0, one launch (start us, length us, event | category | flops | bytes accessed | tf_op | source)
XLA Modules:
  0.0 609.7 jit_solution(7404811745049154196)
XLA Ops:
  15.6 24.6 %all-gather.5.cloned.1.call-done = bf16[128,4096]{1,0:T(8,128)(2,1)} async-done(((bf16[128,1024]{1,0:T(8,128)(2,1)}), bf16[128,4096]{1,0:T(8,128)(2,1)}) %all-gather.5.cloned.1.call-update) | async-done | bytes 1048592 | tf_op jit(solution)/shard_map/all_gather | solution.py:39
  40.3 19.5 %gather_fusion.2 = bf16[1088,4096]{1,0:T(8,128)(2,1)} fusion(bf16[128,4096]{1,0:T(8,128)(2,1)} %all-gather.5.cloned.1.call-done, s32[2048]{0:T(1024)S(1)} %pad_clamp_fusion), kind=kCustom, calls=%fused_computation.1.clone | custom fusion | bytes 17830144 | tf_op jit(solution)/shard_map/jit(_take)/gather | solution.py:28
  59.8 8.2 %select_select_fusion = bf16[1088,4096]{1,0:T(8,128)(2,1)} fusion(bf16[1088,4096]{1,0:T(8,128)(2,1)} %gather_fusion.2, pred[1088]{0:T(1024)(128)(4,1)S(1)} %compare_and_fusion, pred[1088]{0:T(1024)(128)(4,1)S(1)} %fusion.6), kind=kLoop, calls=%fused_computation.6 | loop fusion | flops 8912896 | bytes 17827968 | tf_op jit(solution)/shard_map/jit(_where)/select_n | solution.py:28
  68.0 9.8 %reshape.114 = bf16[16,68,4096]{2,1,0:T(8,128)(2,1)} reshape(bf16[1088,4096]{1,0:T(8,128)(2,1)} %select_select_fusion) | data formatting | bytes 17825792 | tf_op jit(solution)/shard_map/reshape | solution.py:31
  77.8 6.0 all-to-all-start.1
  85.3 28.9 %all-gather.3.cloned.1.call-done = bf16[128,4096]{1,0:T(8,128)(2,1)} async-done(((bf16[128,1024]{1,0:T(8,128)(2,1)}), bf16[128,4096]{1,0:T(8,128)(2,1)}) %all-gather.3.cloned.1.call-update) | async-done | bytes 1048592 | tf_op jit(solution)/shard_map/all_gather | solution.py:40
  114.2 19.5 %gather_fusion.1 = bf16[1088,4096]{1,0:T(8,128)(2,1)} fusion(bf16[128,4096]{1,0:T(8,128)(2,1)} %all-gather.3.cloned.1.call-done, s32[2048]{0:T(1024)S(1)} %pad_clamp_fusion), kind=kCustom, calls=%fused_computation.clone | custom fusion | bytes 17830144 | tf_op jit(solution)/shard_map/jit(_take)/gather | solution.py:29
  133.8 10.1 %select_convert_fusion = bf16[1088,4096]{1,0:T(8,128)(2,1)} fusion(bf16[1088,4096]{1,0:T(8,128)(2,1)} %gather_fusion.1, f32[1088]{0:T(1024)S(1)} %select_reduce_fusion.1, pred[1088]{0:T(1024)(128)(4,1)S(1)} %compare_and_fusion, pred[1088]{0:T(1024)(128)(4,1)S(1)} %fusion.6), kind=kLoop, calls=%fused_computation.3 | loop fusion | flops 22282240 | bytes 17832320 | tf_op jit(solution)/shard_map/convert_element_type | solution.py:30
  143.8 9.8 %reshape.113 = bf16[16,68,4096]{2,1,0:T(8,128)(2,1)} reshape(bf16[1088,4096]{1,0:T(8,128)(2,1)} %select_convert_fusion) | data formatting | bytes 17825792 | tf_op jit(solution)/shard_map/reshape | solution.py:31
  153.7 34.6 %all-to-all-done.1 = bf16[16,68,4096]{2,1,0:T(8,128)(2,1)} async-done(((bf16[16,68,4096]{2,1,0:T(8,128)(2,1)}), bf16[16,68,4096]{2,1,0:T(8,128)(2,1)}, u32[]{:S(2)}, u32[]{:S(2)}) %all-to-all-start.1) | async-done | bytes 8912928 | tf_op jit(solution)/shard_map/all_to_all | solution.py:44
  188.3 5.8 all-to-all-start
  194.3 10.6 %constant_dynamic-update-slice_fusion.1 = bf16[4,4096,768]{2,1,0:T(8,128)(2,1)} fusion(bf16[4,4096,384]{2,1,0:T(8,128)(2,1)} %param.13), kind=kLoop, calls=%fused_computation.47 | loop fusion | bytes 25165824
  204.9 10.6 %constant_dynamic-update-slice_fusion = bf16[4,4096,768]{2,1,0:T(8,128)(2,1)} fusion(bf16[4,4096,768]{2,1,0:T(8,128)(2,1)} %constant_dynamic-update-slice_fusion.1, bf16[4,4096,384]{2,1,0:T(8,128)(2,1)} %param.14), kind=kLoop, calls=%fused_computation.46 | loop fusion | bytes 25165824 | tf_op jit(solution)/shard_map/concatenate | solution.py:47
  215.4 12.8 %copy.66 = bf16[4,4,68,4096]{3,0,2,1:T(4,128)(2,1)} copy(bf16[4,4,68,4096]{3,2,0,1:T(8,128)(2,1)} %bitcast.6) | data formatting | bytes 17825792 | tf_op jit(solution)/shard_map/all_to_all | solution.py:44
  228.2 70.2 %all-to-all-done = bf16[16,68,4096]{2,1,0:T(8,128)(2,1)} async-done(((bf16[16,68,4096]{2,1,0:T(8,128)(2,1)}), bf16[16,68,4096]{2,1,0:T(8,128)(2,1)}, u32[]{:S(2)}, u32[]{:S(2)}) %all-to-all-start) | async-done | bytes 8912928 | tf_op jit(solution)/shard_map/all_to_all | solution.py:45
  298.5 12.8 %copy.64 = bf16[4,4,68,4096]{3,0,2,1:T(4,128)(2,1)} copy(bf16[4,4,68,4096]{3,2,0,1:T(8,128)(2,1)} %bitcast.3) | data formatting | bytes 17825792 | tf_op jit(solution)/shard_map/all_to_all | solution.py:45
  311.3 27.2 %fusion.1 = f32[4,272,768]{2,1,0:T(8,128)S(1)} fusion(bf16[4,4096,768]{2,1,0:T(8,128)(2,1)} %constant_dynamic-update-slice_fusion, bf16[4,272,4096]{2,0,1:T(4,128)(2,1)} %bitcast.46), kind=kOutput, calls=%fused_computation.9 | convolution fusion | flops 6845104128 | bytes 37421056 | tf_op jit(solution)/shard_map/erd,edf->erf/dot_general | solution.py:48
  338.6 23.1 %multiply_convert_fusion.2 = (bf16[4,272,384]{2,1,0:T(8,128)(2,1)}, bf16[4,272,384]{2,1,0:T(8,128)(2,1)}) fusion(f32[4,272,768]{2,1,0:T(8,128)S(1)} %fusion.1, bf16[4,384,4096]{2,1,0:T(8,128)(2,1)} %param.15, bf16[4,272,4096]{2,0,1:T(4,128)(2,1)} %bitcast.42), kind=kOutput, calls=%fused_computation.24 | convolution fusion | flops 3427983360 | bytes 26509312 | tf_op jit(solution)/shard_map/erd,efd->erf/dot_general | solution.py:59
  361.7 16.6 %convert_bitcast_fusion = bf16[4096,4,272]{0,2,1:T(8,128)(2,1)} fusion(bf16[4,4096,768]{2,1,0:T(8,128)(2,1)} %constant_dynamic-update-slice_fusion, bf16[4,272,384]{2,1,0:T(8,128)(2,1)} %get-tuple-element.8, bf16[4,272,384]{2,1,0:T(8,128)(2,1)} %get-tuple-element.7), kind=kOutput, calls=%fused_computation.7 | convolution fusion | flops 6852902912 | bytes 35749888 | tf_op jit(solution)/shard_map/edf,erf->der/dot_general | solution.py:71
  379.7 20.1 %convolution_convert_fusion = bf16[4,4096,768]{2,1,0:T(8,128)(2,1)} fusion(bf16[4,272,4096]{2,0,1:T(4,128)(2,1)} %bitcast.47, bf16[4,272,384]{2,1,0:T(8,128)(2,1)S(1)} %copy-done.6, bf16[4,272,384]{2,1,0:T(8,128)(2,1)S(1)} %copy-done.5), kind=kOutput, calls=%fused_computation.4 | convolution fusion | flops 6861029376 | bytes 35749888 | tf_op jit(solution)/shard_map/erd,erf->edf/dot_general | solution.py:65
  399.8 130.0 %reduce-scatter.2.cloned.1.call-done = bf16[1024,4,272]{0,2,1:T(8,128)(2,1)} async-done(((bf16[4096,4,272]{0,2,1:T(8,128)(2,1)}), bf16[1024,4,272]{0,2,1:T(8,128)(2,1)}) %reduce-scatter.2.cloned.1.call-update) | async-done | bytes 2228240 | tf_op jit(solution)/shard_map/reduce_scatter | solution.py:70
  539.4 19.2 %fusion.20 = (bf16[4,4096,384]{2,1,0:T(8,128)(2,1)}, bf16[4,4096,384]{2,1,0:T(8,128)(2,1)}) fusion(bf16[4,4096,768]{2,1,0:T(8,128)(2,1)} %convolution_convert_fusion), kind=kLoop, calls=%fused_computation.56 | loop fusion | bytes 50331648 | tf_op jit(solution)/shard_map/slice | solution.py:69
  558.6 18.8 %convolution_convert_fusion.1 = bf16[4,384,4096]{2,1,0:T(8,128)(2,1)} fusion(bf16[4,272,4096]{2,0,1:T(4,128)(2,1)S(1)} %bitcast.45, f32[4,272,768]{2,1,0:T(8,128)} %copy-done.4), kind=kOutput, calls=%fused_computation.5 | convolution fusion | flops 3431350272 | bytes 24838144 | tf_op jit(solution)/shard_map/erf,erd->efd/dot_general | solution.py:56
  590.1 8.6 %gather_fusion = f32[1024,1024]{1,0:T(8,128)} fusion(f32[1088,1024]{1,0:T(8,128)} %reshape.115, s32[1024]{0:T(1024)S(1)} %broadcast_clamp_fusion), kind=kCustom, calls=%fused_computation.2 | custom fusion | bytes 8392704 | tf_op jit(solution)/shard_map/jit(_take)/gather | solution.py:81
  (65 shorter events, 37.9 us)
Async XLA Ops:
  7.2 33.1 %all-gather.5.cloned.1.call-start = ((), (), s32[]{:S(2)}) async-start(), calls=%async_computation.5 | async-start | bytes 1310720 | tf_op jit(solution)/shard_map/all_gather | solution.py:39
  13.9 0.6 copy-start
  77.8 6.8 %copy-start.3 = (f32[128,8]{0,1:T(8,128)S(1)}, f32[128,8]{0,1:T(8,128)}, u32[]{:S(2)}) copy-start(f32[128,8]{0,1:T(8,128)} %param.12) | copy-start | bytes 12292
  77.8 110.4 %all-to-all-start.1 = ((bf16[16,68,4096]{2,1,0:T(8,128)(2,1)}), bf16[16,68,4096]{2,1,0:T(8,128)(2,1)}, u32[]{:S(2)}, u32[]{:S(2)}) async-start(bf16[16,68,4096]{2,1,0:T(8,128)(2,1)} %reshape.114), calls=%async_computation.1 | async-start | bytes 18874368 | tf_op jit(solution)/shard_map/all_to_all | solution.py:44
  83.8 30.4 %all-gather.3.cloned.1.call-start = ((), (), s32[]{:S(2)}) async-start(), calls=%async_computation.4 | async-start | bytes 1310720 | tf_op jit(solution)/shard_map/all_gather | solution.py:40
  188.3 110.2 %all-to-all-start = ((bf16[16,68,4096]{2,1,0:T(8,128)(2,1)}), bf16[16,68,4096]{2,1,0:T(8,128)(2,1)}, u32[]{:S(2)}, u32[]{:S(2)}) async-start(bf16[16,68,4096]{2,1,0:T(8,128)(2,1)} %reshape.113), calls=%async_computation | async-start | bytes 18874368 | tf_op jit(solution)/shard_map/all_to_all | solution.py:45
  194.1 335.8 %reduce-scatter.2.cloned.1.call-start = ((), (), s32[]{:S(2)}) async-start(), calls=%async_computation.6 | async-start | bytes 11141120 | tf_op jit(solution)/shard_map/reduce_scatter | solution.py:70
  338.6 23.2 %copy-start.4 = (f32[4,272,768]{2,1,0:T(8,128)}, f32[4,272,768]{2,1,0:T(8,128)S(1)}, u32[]{:S(2)}) copy-start(f32[4,272,768]{2,1,0:T(8,128)S(1)} %fusion.1) | copy-start | bytes 10027012
  378.3 0.7 copy-start.1
  378.3 0.8 copy-start.2
  378.3 1.2 copy-start.5
  378.3 1.4 copy-start.6
  534.5 24.1 %slice-start = ((s8[8912896]{0:T(1024)(128)(4,1)}), s8[524288]{0:T(1024)(128)(4,1)S(1)}, s32[]{:S(2)}) async-start(s8[8912896]{0:T(1024)(128)(4,1)} %bitcast.43), calls=%async_computation.7 | async-start | bytes 1048576
  534.5 42.9 %all-to-all-start.2 = ((bf16[4,272,1024]{2,0,1:T(4,128)(2,1)}), bf16[4,272,1024]{2,0,1:T(4,128)(2,1)}, u32[]{:S(2)}, u32[]{:S(2)}) async-start(bf16[4,272,1024]{2,0,1:T(4,128)(2,1)} %copy.68), calls=%async_computation.3 | async-start | bytes 4456448 | tf_op jit(solution)/shard_map/all_to_all | solution.py:79
  539.3 19.3 %slice-start.1 = ((s8[8912896]{0:T(1024)(128)(4,1)}), s8[4194304]{0:T(1024)(128)(4,1)S(1)}, s32[]{:S(2)}) async-start(s8[8912896]{0:T(1024)(128)(4,1)} %bitcast.43), calls=%async_computation.8 | async-start | bytes 8388608
  539.3 19.3 %slice-start.2 = ((s8[8912896]{0:T(1024)(128)(4,1)}), s8[4194304]{0:T(1024)(128)(4,1)S(1)}, s32[]{:S(2)}) async-start(s8[8912896]{0:T(1024)(128)(4,1)} %bitcast.43), calls=%async_computation.9 | async-start | bytes 8388608
Sparse Core Ops, SparseCore 0:
  9.6 30.6 all-gather.4
  86.3 27.9 all-gather.2
  378.5 151.3 reduce-scatter.1
where the time goes:
time: 617 us; the launch traced here: 610 us
  waiting for transfers between devices  289 us (47%)
  local copies, waits for them, and re-layouts  151 us (24%)
  matrix products  106 us (17%)
  other arithmetic  31.9 us (5%)
  starting transfers between devices  17.3 us (3%)
  between operations  14.1 us (2%)
    reduce_scatter x1, waiting for transfers between devices, per_device(): lax.psum_scatter(jnp.einsum('edf,erf->der', both_weights, both_grads, pre...  130 us
    all_to_all x1, waiting for transfers between devices, per_device(): lax.all_to_all(send_g, 'blk', split_axis=0, concat_axis=1, tiled=True)  70.2 us
    all_to_all x1, waiting for transfers between devices, per_device(): lax.all_to_all(send_x, 'blk', split_axis=0, concat_axis=1, tiled=True)  34.6 us
    all_gather x1, waiting for transfers between devices, per_device(): lax.all_gather(grad_out, 'hid', axis=1, tiled=True)  28.9 us
    dot_general x1, matrix products, per_device(): jnp.einsum('erd,edf->erf', recv_x, both_weights, preferred_element_type=j...  27.2 us
    all_gather x1, waiting for transfers between devices, per_device(): lax.all_gather(tokens, 'hid', axis=1, tiled=True)  24.6 us
    dot_general x1, matrix products, per_device(): jnp.einsum('erd,efd->erf', recv_g, down_w, preferred_element_type=jnp.flo...  23.1 us
    dot_general x1, matrix products, per_device(): jnp.einsum('erd,erf->edf', recv_x, both_grads, preferred_element_type=jnp...  20.1 us
  transfers between devices with their start and end apart: 6, of which 5 were waited for; matrix products, arithmetic and copies ran while one was open for 23% of the time, Pallas kernels for 0%

commit v1 on v0

--- a/solution.py
+++ b/solution.py
@@ -1,6 +1,9 @@
+import functools
 import jax
 import jax.numpy as jnp
 from jax import lax
+from jax.experimental import pallas as pl
+from jax.experimental.pallas import tpu as pltpu
 from jax.sharding import PartitionSpec as P
 
 TOP = 8
@@ -31,7 +34,7 @@
     return (slot_x.reshape(EXPERTS, CAP, width), slot_g.reshape(EXPERTS, CAP, width))
 
 
-def per_device(tokens, grad_out, expert_ids, route_probs, gate_w, up_w, down_w):
+def by_slots(tokens, grad_out, expert_ids, route_probs, gate_w, up_w, down_w):
     local_tokens = tokens.shape[0]
     hidden_part = gate_w.shape[2]
     target, token_of, weight_of, filled = route_tables(expert_ids, route_probs)
@@ -82,6 +85,222 @@
     grad_tokens = jnp.sum(picked, axis=1).astype(jnp.bfloat16)
     return (grad_tokens, grad_gate, grad_up, grad_down)
 
+TILE = 1024
+VMEM_ROOM = 60 * 1024 * 1024
+ROWS_ROWS = (((0,), (0,)), ((), ()))
+COLS_COLS = (((1,), (1,)), ((), ()))
+
+
+def matmul(a, b, dims=(((1,), (0,)), ((), ()))):
+    return lax.dot_general(a, b, dims, preferred_element_type=jnp.float32)
+
+
+def expert_kernel(
+    half, x_ref, g_ref, slot_ref, prob_ref, gate_ref, up_ref, down_ref,
+    dx_ref, ggate_ref, gup_ref, gdown_ref,
+    rows_x, rows_g, gate_sum, up_sum, dh_sum, token_dx, out_gate, out_up, out_down, sems,
+):
+    expert = pl.program_id(0)
+    last = pl.num_programs(0) - 1
+    width = x_ref.shape[1]
+    many = x_ref.shape[0]
+    depth = many // 2
+    hidden_part = gate_ref.shape[2]
+
+    def copies(index):
+        return (
+            pltpu.make_async_copy(out_down, gdown_ref.at[index], sems.at[0]),
+            pltpu.make_async_copy(out_gate, ggate_ref.at[index], sems.at[1]),
+            pltpu.make_async_copy(out_up, gup_ref.at[index], sems.at[2]),
+        )
+
+    slots = slot_ref[0]
+    probs = prob_ref[0]
+    places = []
+    weights = []
+    for part in range(2):
+        match = slots[:, part * depth:(part + 1) * depth] == lax.broadcasted_iota(
+            jnp.int32, (half, depth), 0
+        )
+        weights.append(
+            jnp.sum(jnp.where(match, probs[:, part * depth:(part + 1) * depth], 0.0), axis=1, keepdims=True)
+        )
+        places.append(jnp.where(match, 1.0, 0.0).astype(jnp.bfloat16))
+    weight = jnp.concatenate(weights, axis=0)
+
+    gate_sum[...] = jnp.zeros_like(gate_sum)
+    up_sum[...] = jnp.zeros_like(up_sum)
+    dh_sum[...] = jnp.zeros_like(dh_sum)
+
+    @pl.loop(0, width // TILE)
+    def _(step):
+        cols = pl.ds(pl.multiple_of(step * TILE, TILE), TILE)
+        x_tile = jnp.concatenate(
+            [matmul(places[p], x_ref[p * depth:(p + 1) * depth, cols]) for p in range(2)], axis=0
+        ).astype(jnp.bfloat16)
+        g_tile = (
+            weight
+            * jnp.concatenate(
+                [matmul(places[p], g_ref[p * depth:(p + 1) * depth, cols]) for p in range(2)], axis=0
+            )
+        ).astype(jnp.bfloat16)
+        rows_x[:, cols] = x_tile
+        rows_g[:, cols] = g_tile
+        gate_sum[...] += matmul(x_tile, gate_ref[0, cols, :])
+        up_sum[...] += matmul(x_tile, up_ref[0, cols, :])
+        dh_sum[...] += matmul(g_tile, down_ref[0, :, cols], COLS_COLS)
+
+    gate_value = gate_sum[...]
+    up_value = up_sum[...]
+    d_hidden = dh_sum[...]
+    sigmoid_gate = jax.nn.sigmoid(gate_value)
+    activated = gate_value * sigmoid_gate
+    hidden = (activated * up_value).astype(jnp.bfloat16)
+    d_gate_h = (
+        d_hidden * up_value * sigmoid_gate * (1.0 + gate_value * (1.0 - sigmoid_gate))
+    ).astype(jnp.bfloat16)
+    d_up_h = (d_hidden * activated).astype(jnp.bfloat16)
+    d_both = jnp.concatenate((d_gate_h, d_up_h), axis=1)
+
+    @pl.when(expert > 0)
+    def _():
+        for copy in copies(expert - 1):
+            copy.wait()
+
+    @pl.loop(0, width // TILE)
+    def _(step):
+        cols = pl.ds(pl.multiple_of(step * TILE, TILE), TILE)
+        out_down[:, cols] = matmul(hidden, rows_g[:, cols], ROWS_ROWS).astype(jnp.bfloat16)
+        both = matmul(rows_x[:, cols], d_both, ROWS_ROWS).astype(jnp.bfloat16)
+        out_gate[cols, :] = both[:, :hidden_part]
+        out_up[cols, :] = both[:, hidden_part:]
+        slot_dx = matmul(d_gate_h, gate_ref[0, cols, :], COLS_COLS) + matmul(
+            d_up_h, up_ref[0, cols, :], COLS_COLS
+        )
+        for p in range(2):
+            term = matmul(
+                places[p], slot_dx[p * half:(p + 1) * half].astype(jnp.bfloat16), ROWS_ROWS
+            )
+            area = (slice(p * depth, (p + 1) * depth), cols)
+
+            @pl.when(expert == 0)
+            def _():
+                token_dx[area] = term
+
+            @pl.when((expert > 0) & (expert < last))
+            def _():
+                token_dx[area] += term
+
+            @pl.when((expert > 0) & (expert == last))
+            def _():
+                dx_ref[area] = (token_dx[area] + term).astype(jnp.bfloat16)
+
+    for copy in copies(expert):
+        copy.start()
+
+    @pl.when(expert == last)
+    def _():
+        for copy in copies(expert):
+            copy.wait()
+
+
+def expert_pass(all_x, all_g, slots, probs, gate_w, up_w, down_w, half):
+    experts, width, hidden_part = gate_w.shape
+    many = all_x.shape[0]
+    rows = 2 * half
+    whole = pl.BlockSpec((many, width), lambda e: (0, 0), pipeline_mode=pl.Buffered(1))
+    line = pl.BlockSpec((1, 1, many), lambda e: (e, 0, 0))
+    weight_in = pl.BlockSpec((1, width, hidden_part), lambda e: (e, 0, 0))
+    weight_out = pl.BlockSpec((1, hidden_part, width), lambda e: (e, 0, 0))
+    bf16 = jnp.bfloat16
+    return pl.pallas_call(
+        functools.partial(expert_kernel, half),
+        grid=(experts,),
+        in_specs=[whole, whole, line, line, weight_in, weight_in, weight_out],
+        out_specs=[
+            pl.BlockSpec((many, width), lambda e: (0, 0)),
+            pl.BlockSpec(memory_space=pl.ANY),
+            pl.BlockSpec(memory_space=pl.ANY),
+            pl.BlockSpec(memory_space=pl.ANY),
+        ],
+        out_shape=[
+            jax.ShapeDtypeStruct((many, width), bf16),
+            jax.ShapeDtypeStruct(gate_w.shape, bf16),
+            jax.ShapeDtypeStruct(up_w.shape, bf16),
+            jax.ShapeDtypeStruct(down_w.shape, bf16),
+        ],
+        scratch_shapes=[
+            pltpu.VMEM((rows, width), bf16),
+            pltpu.VMEM((rows, width), bf16),
+            pltpu.VMEM((rows, hidden_part), jnp.float32),
+            pltpu.VMEM((rows, hidden_part), jnp.float32),
+            pltpu.VMEM((rows, hidden_part), jnp.float32),
+            pltpu.VMEM((many, width), jnp.float32),
+            pltpu.VMEM((width, hidden_part), bf16),
+            pltpu.VMEM((width, hidden_part), bf16),
+            pltpu.VMEM((hidden_part, width), bf16),
+            pltpu.SemaphoreType.DMA((3,)),
+        ],
+        compiler_params=pltpu.CompilerParams(
+            dimension_semantics=("arbitrary",), vmem_limit_bytes=VMEM_ROOM
+        ),
+        cost_estimate=pl.CostEstimate(
+            flops=16 * experts * rows * width * hidden_part,
+            bytes_accessed=12 * experts * width * hidden_part,
+            transcendentals=experts * rows * hidden_part,
+        ),
+    )(all_x, all_g, slots, probs, gate_w, up_w, down_w)
+
+
+def local_routes(expert_ids, route_probs, experts, depth):
+    ids = lax.all_gather(expert_ids, "blk", axis=0, tiled=True)
+    probs = lax.all_gather(route_probs, "blk", axis=0, tiled=True)
+    first = lax.axis_index("blk") * experts
+    mine = first + jnp.arange(experts, dtype=jnp.int32)
+    same = ids[None, :, :] == mine[:, None, None]
+    member = jnp.any(same, axis=2)
+    prob = jnp.sum(jnp.where(same, probs[None], 0.0), axis=2)
+    many = ids.shape[0]
+    halves = member.astype(jnp.int32).reshape(experts, many // depth, depth)
+    earlier = (jnp.cumsum(halves, axis=2) - halves).reshape(experts, many)
+    slot = jnp.where(member, earlier, -1)
+    return slot.reshape(experts, 1, many), prob.reshape(experts, 1, many)
+
+
+def by_tokens(tokens, grad_out, expert_ids, route_probs, gate_w, up_w, down_w):
+    experts = gate_w.shape[0]
+    n_blk = lax.axis_size("blk")
+    depth = n_blk * tokens.shape[0] // 2
+    half = n_blk * CAP // 2
+    slots, probs = local_routes(expert_ids, route_probs, experts, depth)
+    all_x, all_g = (
+        lax.all_gather(
+            lax.all_gather(part, "hid", axis=1, tiled=True), "blk", axis=0, tiled=True
+        )
+        for part in (tokens, grad_out)
+    )
+    dx, grad_gate, grad_up, grad_down = expert_pass(
+        all_x, all_g, slots, probs, gate_w, up_w, down_w, half
+    )
+    dx = lax.psum_scatter(dx, "blk", scatter_dimension=0, tiled=True)
+    grad_tokens = lax.psum_scatter(dx, "hid", scatter_dimension=1, tiled=True)
+    return (grad_tokens, grad_gate, grad_up, grad_down)
+
+
+def fits(many, width, hidden_part, experts, n_blk):
+    rows = n_blk * CAP
+    held = 2 * (2 * 3 + 3) * width * hidden_part + (2 * 2 + 2 * 2 + 4) * many * width
+    held += 4 * rows * width + 12 * rows * hidden_part
+    aligned = hidden_part % 128 == 0 and width % TILE == 0 and n_blk % 4 == 0
+    return aligned and experts > 1 and (many // 2) % 128 == 0 and held < VMEM_ROOM
+
+
+def per_device(tokens, grad_out, expert_ids, route_probs, gate_w, up_w, down_w):
+    n_blk = lax.axis_size("blk")
+    experts, width, hidden_part = gate_w.shape
+    plan = by_tokens if fits(n_blk * tokens.shape[0], width, hidden_part, experts, n_blk) else by_slots
+    return plan(tokens, grad_out, expert_ids, route_probs, gate_w, up_w, down_w)
+
 
 def solution(mesh):
     placed = (

time: 617 us -> 309 us (0.50); the launches traced: 610 us -> 309 us
  local copies, waits for them, and re-layouts: 151 us -> 0.92 us
  matrix products: 106 us -> 0 us
  waiting for transfers between devices: 289 us -> 193 us
  Pallas kernels: 0 us -> 86.8 us
  other arithmetic: 31.9 us -> 3.36 us
  starting transfers between devices: 17.3 us -> 0.23 us
  blocking collectives: 0 us -> 10.6 us
    dot_general x5 -> x0, matrix products: 106 us -> none  [the longest x1 27.2 us: per_device(): jnp.einsum('erd,edf->erf', recv_x, both_weights, preferred_element_type=j...]
    all_to_all x3 -> x0, waiting for transfers between devices: 105 us -> none  [the longest x1 70.2 us: per_device(): lax.all_to_all(send_g, 'blk', split_axis=0, concat_axis=1, tiled=True)]
    pallas_call x0 -> x1, Pallas kernels: none -> 86.8 us  [expert_pass(): pl.pallas_call(functools.partial(expert_kernel, half), grid=(experts,), i...]
    all_gather x2 -> x4, waiting for transfers between devices: 53.5 us -> 117 us  [the longest x2 60.5 us: by_tokens(): lax.all_gather(part, 'hid', axis=1, tiled=True)]
    reduce_scatter x1 -> x2, waiting for transfers between devices: 130 us -> 74.6 us  [the longest x1 44.6 us: by_tokens(): dx = lax.psum_scatter(dx, 'blk', scatter_dimension=0, tiled=True)]
    gather x3 -> x0, local copies, waits for them, and re-layouts: 47.7 us -> none  [the longest x1 19.5 us: place_rows(): slot_x = jnp.where(filled[:, None], jnp.take(features, token_of, axis=0), 0)]
    all_to_all x2 -> x0, local copies, waits for them, and re-layouts: 25.6 us -> none  [the longest x1 12.8 us: per_device(): lax.all_to_all(send_g, 'blk', split_axis=0, concat_axis=1, tiled=True)]
    slice x3 -> x2, local copies, waits for them, and re-layouts: 19.4 us -> 0.19 us  [the longest x1 19.2 us: per_device(): grad_up = weight_grads[:, :, hidden_part:]]
  transfers between devices with their start and end apart: 6 -> 6, of which waited for: 5 -> 6; matrix products, arithmetic and copies ran while one was open for 23% -> 1% of each run, Pallas kernels for 0% -> 0%
where the time goes in v1:
time: 309 us
  waiting for transfers between devices  193 us (62%)
  Pallas kernels  86.8 us (28%)
  between operations  14.1 us (5%)
  blocking collectives  10.6 us (3%)
  other arithmetic  3.36 us (1%)
    pallas_call x1, Pallas kernels, expert_pass(): pl.pallas_call(functools.partial(expert_kernel, half), grid=(experts,), i...  86.8 us
    all_gather x2, waiting for transfers between devices, by_tokens(): lax.all_gather(part, 'hid', axis=1, tiled=True)  60.5 us
    all_gather x2, waiting for transfers between devices, by_tokens(): lax.all_gather(lax.all_gather(part, 'hid', axis=1, tiled=True), 'blk', ax...  56.6 us
    reduce_scatter x1, waiting for transfers between devices, by_tokens(): dx = lax.psum_scatter(dx, 'blk', scatter_dimension=0, tiled=True)  44.6 us
    reduce_scatter x1, waiting for transfers between devices, by_tokens(): grad_tokens = lax.psum_scatter(dx, 'hid', scatter_dimension=1, tiled=True)  30 us
  transfers between devices with their start and end apart: 6, of which 6 were waited for; matrix products, arithmetic and copies ran while one was open for 1% of the time, Pallas kernels for 0%

profile of v1, /device:TPU:0, one launch (start us, length us, event | category | flops | bytes accessed | tf_op | source)
XLA Modules:
  0.0 309.2 jit_solution(1260473669011558641)
XLA Ops:
  7.2 0.7 all-gather.5.cloned.1.call-update
  7.9 0.0 all-gather.9.cloned.1.call-start
  7.9 0.7 all-gather.9.cloned.1.call-update
  8.6 0.0 all-gather.7.cloned.1.call-start
  8.7 31.5 %all-gather.5.cloned.1.call-done = bf16[128,4096]{1,0:T(8,128)(2,1)} async-done(((bf16[128,1024]{1,0:T(8,128)(2,1)}), bf16[128,4096]{1,0:T(8,128)(2,1)}) %all-gather.5.cloned.1.call-update) | async-done | bytes 1048592 | tf_op jit(solution)/shard_map/all_gather | solution.py:278
  40.3 29.0 %all-gather.9.cloned.1.call-done = bf16[128,4096]{1,0:T(8,128)(2,1)} async-done(((bf16[128,1024]{1,0:T(8,128)(2,1)}), bf16[128,4096]{1,0:T(8,128)(2,1)}) %all-gather.9.cloned.1.call-update) | async-done | bytes 1048592 | tf_op jit(solution)/shard_map/all_gather | solution.py:278
  69.3 0.0 reduce-scatter.3.cloned.1.call-start
  69.3 5.3 %all_gather.22 = s32[512,8]{0,1:T(8,128)S(1)} all-gather(s32[128,8]{0,1:T(8,128)} %param.9), channel_id=1, replica_groups=mesh['grp'=2,'blk'=4,'hid'=4] {'blk'}, dimensions={0}, use_global_device_ids=true | all-gather | bytes 20480 | tf_op jit(solution)/shard_map/all_gather | solution.py:256
  74.7 0.1 compare_reduce_fusion
  74.8 2.4 reduce-window.6
  77.2 0.1 slice.8
  77.3 0.1 copy.21
  77.5 0.1 copy.22
  77.6 5.3 %all_gather.23 = f32[512,8]{0,1:T(8,128)S(1)} all-gather(f32[128,8]{0,1:T(8,128)} %param.10), channel_id=1, replica_groups=mesh['grp'=2,'blk'=4,'hid'=4] {'blk'}, dimensions={0}, use_global_device_ids=true | all-gather | bytes 20480 | tf_op jit(solution)/shard_map/all_gather | solution.py:257
  82.9 0.1 fusion
  83.0 0.6 reshape.66.prob_ref
  83.6 0.1 broadcast_add_fusion
  83.7 0.6 copy_select_fusion.slot_ref
  84.3 20.7 %all-gather.7.cloned.1.call-done.x_ref = bf16[512,4096]{1,0:T(8,128)(2,1)} async-done(((bf16[128,4096]{1,0:T(8,128)(2,1)}), bf16[512,4096]{1,0:T(8,128)(2,1)}) %all-gather.7.cloned.1.call-update) | async-done | bytes 4194320 | tf_op jit(solution)/shard_map/all_gather | solution.py:277
  105.0 35.9 %all-gather.11.cloned.1.call-done.g_ref = bf16[512,4096]{1,0:T(8,128)(2,1)} async-done(((bf16[128,4096]{1,0:T(8,128)(2,1)}), bf16[512,4096]{1,0:T(8,128)(2,1)}) %all-gather.11.cloned.1.call-update) | async-done | bytes 4194320 | tf_op jit(solution)/shard_map/all_gather | solution.py:277
  140.8 86.8 %shard_map.102 = (bf16[512,4096]{1,0:T(8,128)(2,1)}, bf16[4,4096,384]{2,1,0:T(8,128)(2,1)}, bf16[4,4096,384]{2,1,0:T(8,128)(2,1)}, bf16[4,384,4096]{2,1,0:T(8,128)(2,1)}) custom-call(bf16[512,4096]{1,0:T(8,128)(2,1)} %all-gather.7.cloned.1.call-done.x_ref, bf16[512,4096]{1,0:T(8,128)(2,1)} %all-gather.11.cloned.1.call-done.g_ref, ...), custom_call_target="tpu_custom_call" | custom-call | flops 27380416512 | bytes 75497472 | tf_op jit(solution)/shard_map/pallas_call | solution.py:216
  227.7 0.0 reduce-scatter.5.cloned.1.call-start
  227.7 44.6 %reduce-scatter.3.cloned.1.call-done = bf16[128,4096]{1,0:T(8,128)(2,1)} async-done(((bf16[512,4096]{1,0:T(8,128)(2,1)}), bf16[128,4096]{1,0:T(8,128)(2,1)}) %reduce-scatter.3.cloned.1.call-update) | async-done | bytes 1048592 | tf_op jit(solution)/shard_map/reduce_scatter | solution.py:285
  272.4 30.0 %reduce-scatter.5.cloned.1.call-done = bf16[128,1024]{1,0:T(8,128)(2,1)} async-done(((bf16[128,4096]{1,0:T(8,128)(2,1)}), bf16[128,1024]{1,0:T(8,128)(2,1)}) %reduce-scatter.5.cloned.1.call-update) | async-done | bytes 262160 | tf_op jit(solution)/shard_map/reduce_scatter | solution.py:286
  (11 shorter events, 0.2 us)
Async XLA Ops:
  7.2 33.1 %all-gather.5.cloned.1.call-start = ((), (), s32[]{:S(2)}) async-start(), calls=%async_computation.2 | async-start | bytes 1310720 | tf_op jit(solution)/shard_map/all_gather | solution.py:278
  7.9 61.4 %all-gather.9.cloned.1.call-start = ((), (), s32[]{:S(2)}) async-start(), calls=%async_computation.4 | async-start | bytes 1310720 | tf_op jit(solution)/shard_map/all_gather | solution.py:278
  8.6 96.3 %all-gather.7.cloned.1.call-start = ((), (), s32[]{:S(2)}) async-start(), calls=%async_computation.3 | async-start | bytes 5242880 | tf_op jit(solution)/shard_map/all_gather | solution.py:277
  40.3 100.6 %all-gather.11.cloned.1.call-start = ((), (), s32[]{:S(2)}) async-start(), calls=%async_computation.5 | async-start | bytes 5242880 | tf_op jit(solution)/shard_map/all_gather | solution.py:277
  69.3 203.0 %reduce-scatter.3.cloned.1.call-start = ((), (), s32[]{:S(2)}) async-start(), calls=%async_computation.6 | async-start | bytes 5242880 | tf_op jit(solution)/shard_map/reduce_scatter | solution.py:285
  227.7 74.6 %reduce-scatter.5.cloned.1.call-start = ((), (), s32[]{:S(2)}) async-start(), calls=%async_computation.7 | async-start | bytes 1310720 | tf_op jit(solution)/shard_map/reduce_scatter | solution.py:286
Sparse Core Ops, SparseCore 0:
  9.6 30.6 all-gather.4
  41.8 27.4 all-gather.8
  70.8 34.0 all-gather.6
  106.4 34.4 all-gather.10
  227.8 44.4 reduce-scatter.2
  275.2 27.1 reduce-scatter.4

commit v2 on v1

--- a/solution.py
+++ b/solution.py
@@ -86,6 +86,7 @@
     return (grad_tokens, grad_gate, grad_up, grad_down)
 
 TILE = 1024
+MESH = pl.DeviceIdType.MESH
 VMEM_ROOM = 60 * 1024 * 1024
 ROWS_ROWS = (((0,), (0,)), ((), ()))
 COLS_COLS = (((1,), (1,)), ((), ()))
@@ -98,7 +99,7 @@
 def expert_kernel(
     half, x_ref, g_ref, slot_ref, prob_ref, gate_ref, up_ref, down_ref,
     dx_ref, ggate_ref, gup_ref, gdown_ref,
-    rows_x, rows_g, gate_sum, up_sum, dh_sum, token_dx, out_gate, out_up, out_down, sems,
+    rows_x, rows_g, both_sum, dh_sum, token_dx, out_gate, out_up, out_down, sems,
 ):
     expert = pl.program_id(0)
     last = pl.num_programs(0) - 1
@@ -128,8 +129,7 @@
         places.append(jnp.where(match, 1.0, 0.0).astype(jnp.bfloat16))
     weight = jnp.concatenate(weights, axis=0)
 
-    gate_sum[...] = jnp.zeros_like(gate_sum)
-    up_sum[...] = jnp.zeros_like(up_sum)
+    both_sum[...] = jnp.zeros_like(both_sum)
     dh_sum[...] = jnp.zeros_like(dh_sum)
 
     @pl.loop(0, width // TILE)
@@ -146,12 +146,12 @@
         ).astype(jnp.bfloat16)
         rows_x[:, cols] = x_tile
         rows_g[:, cols] = g_tile
-        gate_sum[...] += matmul(x_tile, gate_ref[0, cols, :])
-        up_sum[...] += matmul(x_tile, up_ref[0, cols, :])
+        both_w = jnp.concatenate((gate_ref[0, cols, :], up_ref[0, cols, :]), axis=1)
+        both_sum[...] += matmul(x_tile, both_w)
         dh_sum[...] += matmul(g_tile, down_ref[0, :, cols], COLS_COLS)
 
-    gate_value = gate_sum[...]
-    up_value = up_sum[...]
+    gate_value = both_sum[:, :hidden_part]
+    up_value = both_sum[:, hidden_part:]
     d_hidden = dh_sum[...]
     sigmoid_gate = jax.nn.sigmoid(gate_value)
     activated = gate_value * sigmoid_gate
@@ -174,9 +174,8 @@
         both = matmul(rows_x[:, cols], d_both, ROWS_ROWS).astype(jnp.bfloat16)
         out_gate[cols, :] = both[:, :hidden_part]
         out_up[cols, :] = both[:, hidden_part:]
-        slot_dx = matmul(d_gate_h, gate_ref[0, cols, :], COLS_COLS) + matmul(
-            d_up_h, up_ref[0, cols, :], COLS_COLS
-        )
+        both_w = jnp.concatenate((gate_ref[0, cols, :], up_ref[0, cols, :]), axis=1)
+        slot_dx = matmul(d_both, both_w, COLS_COLS)
         for p in range(2):
             term = matmul(
                 places[p], slot_dx[p * half:(p + 1) * half].astype(jnp.bfloat16), ROWS_ROWS
@@ -232,8 +231,7 @@
         scratch_shapes=[
             pltpu.VMEM((rows, width), bf16),
             pltpu.VMEM((rows, width), bf16),
-            pltpu.VMEM((rows, hidden_part), jnp.float32),
-            pltpu.VMEM((rows, hidden_part), jnp.float32),
+            pltpu.VMEM((rows, 2 * hidden_part), jnp.float32),
             pltpu.VMEM((rows, hidden_part), jnp.float32),
             pltpu.VMEM((many, width), jnp.float32),
             pltpu.VMEM((width, hidden_part), bf16),
@@ -252,18 +250,374 @@
     )(all_x, all_g, slots, probs, gate_w, up_w, down_w)
 
 
-def local_routes(expert_ids, route_probs, experts, depth):
-    ids = lax.all_gather(expert_ids, "blk", axis=0, tiled=True)
-    probs = lax.all_gather(route_probs, "blk", axis=0, tiled=True)
+def greet(blk, hid, n_hid):
+    barrier = pltpu.get_barrier_semaphore()
+    for hop in range(1, 4):
+        pl.semaphore_signal(
+            barrier, inc=1, device_id={"blk": lax.rem(blk + hop, 4)}, device_id_type=MESH
+        )
+
+    @pl.when(hid > 0)
+    def _():
+        pl.semaphore_signal(barrier, inc=1, device_id={"hid": hid - 1}, device_id_type=MESH)
+
+    @pl.when(hid < n_hid - 1)
+    def _():
+        pl.semaphore_signal(barrier, inc=1, device_id={"hid": hid + 1}, device_id_type=MESH)
+
+    below = lax.div(hid + n_hid - 1, n_hid)
+    above = lax.div(2 * n_hid - 2 - hid, n_hid)
+    pl.semaphore_wait(barrier, 3 + below + above)
+
+
+def gather_kernel(
+    n_hid, x_ref, g_ref, ids_ref, prob_ref, all_x, all_g, all_ids, all_prob,
+    own_sems, line_send, x_send, core_send, recv, small_send, small_recv,
+):
+    blk = lax.axis_index("blk")
+    hid = lax.axis_index("hid")
+    rows, part = x_ref.shape
+    sibling = blk + 1 - 2 * lax.rem(blk, 2)
+    across = lax.rem(blk + 2, 4)
+    sources = (x_ref, g_ref)
+    fulls = (all_x, all_g)
+    smalls = ((ids_ref, all_ids), (prob_ref, all_prob))
+
+    def area(which, owner, column):
+        return fulls[which].at[
+            pl.ds(pl.multiple_of(owner * rows, rows), rows),
+            pl.ds(pl.multiple_of(column * part, part), part),
+        ]
+
+    def small_area(which, owner):
+        return smalls[which][1].at[pl.ds(pl.multiple_of(owner * TOP, TOP), TOP), :]
+
+    def push(which, owner, column, sem, device, own=False):
+        return pltpu.make_async_remote_copy(
+            src_ref=sources[which] if own else area(which, owner, column),
+            dst_ref=area(which, owner, column),
+            send_sem=sem,
+            recv_sem=recv.at[which, owner, column],
+            device_id=device,
+            device_id_type=MESH,
+        )
+
+    def up(which, column, own=False):
+        return push(which, blk, column, line_send.at[0, which, column], {"hid": hid + 1}, own)
+
+    def down(which, column, own=False):
+        return push(which, blk, column, line_send.at[1, which, column], {"hid": hid - 1}, own)
+
+    def line_sent(way, which, column):
+        push(which, blk, column, line_send.at[way, which, column], {"blk": sibling}).wait_send()
+
+    def over(which, column, own=False):
+        return push(which, blk, column, x_send.at[which, column], {"blk": across}, own)
+
+    def beside(which, index, column, own=False):
+        owner = (blk, across)[index]
+        return push(which, owner, column, core_send.at[index, which, column], {"blk": sibling}, own)
+
+    def small(which, hop):
+        return pltpu.make_async_remote_copy(
+            src_ref=smalls[which][0],
+            dst_ref=small_area(which, blk),
+            send_sem=small_send.at[which, hop],
+            recv_sem=small_recv.at[which, hop],
+            device_id={"blk": lax.rem(blk + hop, 4)},
+            device_id_type=MESH,
+        )
+
+    def landed(which, owner, column):
+        push(which, owner, column, recv.at[which, owner, column], {"blk": sibling}).wait_recv()
+
+    def keep():
+        return [
+            pltpu.make_async_copy(sources[w], area(w, blk, hid), own_sems.at[w]) for w in range(2)
+        ] + [
+            pltpu.make_async_copy(smalls[w][0], small_area(w, blk), own_sems.at[2 + w])
+            for w in range(2)
+        ]
+
+    def from_across(step):
+        for side in (-1, 1) if step else (1,):
+            column = hid + side * step
+
+            @pl.when((column >= 0) & (column < n_hid))
+            def _():
+                for which in range(2):
+                    landed(which, across, column)
+                    beside(which, 1, column).start()
+
+    greet(blk, hid, n_hid)
+    for which in range(2):
+        @pl.when(hid < n_hid - 1)
+        def _():
+            up(which, hid, True).start()
+
+        @pl.when(hid > 0)
+        def _():
+            down(which, hid, True).start()
+
+        over(which, hid, True).start()
+    for which in range(2):
+        beside(which, 0, hid, True).start()
+        for hop in range(1, 4):
+            small(which, hop).start()
+    for copy in keep():
+        copy.start()
+    for step in range(1, n_hid):
+        @pl.when(hid - step >= 0)
+        def _():
+            column = hid - step
+            for which in range(2):
+                landed(which, blk, column)
+
+                @pl.when(hid < n_hid - 1)
+                def _():
+                    up(which, column).start()
+
+                over(which, column).start()
+                beside(which, 0, column).start()
+
+        @pl.when(hid + step < n_hid)
+        def _():
+            column = hid + step
+            for which in range(2):
+                landed(which, blk, column)
+
+                @pl.when(hid > 0)
+                def _():
+                    down(which, column).start()
+
+                over(which, column).start()
+                beside(which, 0, column).start()
+
+        from_across(step - 1)
+    from_across(n_hid - 1)
+
+    beyond = lax.rem(sibling + 2, 4)
+    for column in range(n_hid):
+        for which in range(2):
+            landed(which, sibling, column)
+            landed(which, beyond, column)
+            over(which, column).wait_send()
+            beside(which, 0, column).wait_send()
+            beside(which, 1, column).wait_send()
+
+            @pl.when((hid >= column) & (hid < n_hid - 1))
+            def _():
+                line_sent(0, which, column)
+
+            @pl.when((hid <= column) & (hid > 0))
+            def _():
+                line_sent(1, which, column)
+
+    for which in range(2):
+        for hop in range(1, 4):
+            small(which, hop).wait()
+    for copy in keep():
+        copy.wait()
+
+
+def gather_all(tokens, grad_out, ids, probs, n_hid):
+    rows, part = tokens.shape
+    anywhere = pl.BlockSpec(memory_space=pl.ANY)
+    full = jax.ShapeDtypeStruct((4 * rows, n_hid * part), tokens.dtype)
+    dma = pltpu.SemaphoreType.DMA
+    return pl.pallas_call(
+        functools.partial(gather_kernel, n_hid),
+        in_specs=[anywhere] * 4,
+        out_specs=[anywhere] * 4,
+        out_shape=[
+            full,
+            full,
+            jax.ShapeDtypeStruct((4 * ids.shape[0], ids.shape[1]), ids.dtype),
+            jax.ShapeDtypeStruct((4 * probs.shape[0], probs.shape[1]), probs.dtype),
+        ],
+        scratch_shapes=[
+            dma((4,)),
+            dma((2, 2, n_hid)),
+            dma((2, n_hid)),
+            dma((2, 2, n_hid)),
+            dma((2, 4, n_hid)),
+            dma((2, 4)),
+            dma((2, 4)),
+        ],
+        compiler_params=pltpu.CompilerParams(collective_id=1, has_side_effects=True),
+    )(tokens, grad_out, ids, probs)
+
+
+def reduce_kernel(
+    n_hid, dx_ref, out_ref, core_in, x_out, x_in, line_out, line_in,
+    core_send, core_recv, x_send, x_recv, line_send, line_recv,
+):
+    blk = lax.axis_index("blk")
+    hid = lax.axis_index("hid")
+    rows, part = out_ref.shape
+    sibling = blk + 1 - 2 * lax.rem(blk, 2)
+    across = lax.rem(blk + 2, 4)
+    beyond = lax.rem(sibling + 2, 4)
+
+    def area(owner, column):
+        return dx_ref.at[
+            pl.ds(pl.multiple_of(owner * rows, rows), rows),
+            pl.ds(pl.multiple_of(column * part, part), part),
+        ]
+
+    def wide(ref):
+        return ref[...].astype(jnp.float32)
+
+    def push(src, dst, send, recv, device):
+        return pltpu.make_async_remote_copy(
+            src_ref=src, dst_ref=dst, send_sem=send, recv_sem=recv,
+            device_id=device, device_id_type=MESH,
+        )
+
+    def beside(index, column):
+        return push(
+            area((sibling, beyond)[index], column), core_in.at[index, column],
+            core_send.at[index, column], core_recv.at[index, column], {"blk": sibling},
+        )
+
+    def over(column):
+        return push(
+            x_out.at[column], x_in.at[column], x_send.at[column], x_recv.at[column], {"blk": across}
+        )
+
+    def along(way, column):
+        return push(
+            line_out.at[column], line_in.at[way, column],
+            line_send.at[column], line_recv.at[way, column], {"hid": hid + (1, -1)[way]},
+        )
+
+    def arrived(way, column):
+        push(
+            line_out.at[column], line_in.at[way, column],
+            line_send.at[column], line_recv.at[way, column], {"blk": sibling},
+        ).wait_recv()
+
+    def line_sent(column):
+        push(
+            line_out.at[column], line_in.at[0, column],
+            line_send.at[column], line_recv.at[0, column], {"blk": sibling},
+        ).wait_send()
+
+    def each(body):
+        for step in range(n_hid - 1, 0, -1):
+            for side in (1, -1):
+                column = hid + side * step
+
+                @pl.when((column >= 0) & (column < n_hid))
+                def _():
+                    body(column, side)
+
+        body(hid, 0)
+
+    def send_core(column, side):
+        beside(1, column).start()
+        beside(0, column).start()
+
+    def send_x(column, side):
+        beside(1, column).wait_recv()
+        x_out[column] = (wide(area(across, column)) + wide(core_in.at[1, column])).astype(x_out.dtype)
+        over(column).start()
+
+    def send_line(column, side):
+        beside(0, column).wait_recv()
+        over(column).wait_recv()
+        near = wide(area(blk, column)) + wide(core_in.at[0, column]) + wide(x_in.at[column])
+        if side:
+            way = 0 if side == 1 else 1
+            inner = hid > 0 if side == 1 else hid < n_hid - 1
+
+            @pl.when(inner)
+            def _():
+                arrived(way, column)
+                line_out[column] = (near + wide(line_in.at[way, column])).astype(line_out.dtype)
+
+            @pl.when(jnp.logical_not(inner))
+            def _():
+                line_out[column] = near.astype(line_out.dtype)
+
+            along(way, column).start()
+            return
+
+        @pl.when(hid == 0)
+        def _():
+            arrived(1, column)
+            out_ref[...] = (near + wide(line_in.at[1, column])).astype(out_ref.dtype)
+
+        @pl.when(hid == n_hid - 1)
+        def _():
+            arrived(0, column)
+            out_ref[...] = (near + wide(line_in.at[0, column])).astype(out_ref.dtype)
+
+        @pl.when((hid > 0) & (hid < n_hid - 1))
+        def _():
+            arrived(0, column)
+            arrived(1, column)
+            out_ref[...] = (
+                near + wide(line_in.at[0, column]) + wide(line_in.at[1, column])
+            ).astype(out_ref.dtype)
+
+    greet(blk, hid, n_hid)
+    each(send_core)
+    each(send_x)
+    each(send_line)
+    for column in range(n_hid):
+        beside(0, column).wait_send()
+        beside(1, column).wait_send()
+        over(column).wait_send()
+
+        @pl.when(hid != column)
+        def _():
+            line_sent(column)
+
+
+def reduce_all(dx, rows, part, n_hid):
+    bf16 = jnp.bfloat16
+    dma = pltpu.SemaphoreType.DMA
+    inside = pl.BlockSpec(memory_space=pltpu.VMEM)
+    return pl.pallas_call(
+        functools.partial(reduce_kernel, n_hid),
+        in_specs=[inside],
+        out_specs=inside,
+        out_shape=jax.ShapeDtypeStruct((rows, part), bf16),
+        scratch_shapes=[
+            pltpu.VMEM((2, n_hid, rows, part), bf16),
+            pltpu.VMEM((n_hid, rows, part), bf16),
+            pltpu.VMEM((n_hid, rows, part), bf16),
+            pltpu.VMEM((n_hid, rows, part), bf16),
+            pltpu.VMEM((2, n_hid, rows, part), bf16),
+            dma((2, n_hid)),
+            dma((2, n_hid)),
+            dma((n_hid,)),
+            dma((n_hid,)),
+            dma((n_hid,)),
+            dma((2, n_hid)),
+        ],
+        compiler_params=pltpu.CompilerParams(
+            collective_id=2, has_side_effects=True, vmem_limit_bytes=40 * 1024 * 1024
+        ),
+    )(dx)
+
+
+def local_routes(ids, probs, experts, depth):
     first = lax.axis_index("blk") * experts
     mine = first + jnp.arange(experts, dtype=jnp.int32)
-    same = ids[None, :, :] == mine[:, None, None]
-    member = jnp.any(same, axis=2)
-    prob = jnp.sum(jnp.where(same, probs[None], 0.0), axis=2)
-    many = ids.shape[0]
-    halves = member.astype(jnp.int32).reshape(experts, many // depth, depth)
-    earlier = (jnp.cumsum(halves, axis=2) - halves).reshape(experts, many)
-    slot = jnp.where(member, earlier, -1)
+    groups = ids.shape[0] // TOP
+    many = groups * ids.shape[1]
+    same = ids.reshape(1, groups, TOP, -1) == mine[:, None, None, None]
+    member = jnp.any(same, axis=2).reshape(experts, many)
+    prob = jnp.sum(jnp.where(same, probs.reshape(1, groups, TOP, -1), 0.0), axis=2)
+    before = jnp.arange(depth)[:, None] < jnp.arange(depth)[None, :]
+    earlier = jnp.dot(
+        member.reshape(-1, depth).astype(jnp.bfloat16),
+        before.astype(jnp.bfloat16),
+        preferred_element_type=jnp.float32,
+    ).reshape(experts, many)
+    slot = jnp.where(member, earlier.astype(jnp.int32), -1)
     return slot.reshape(experts, 1, many), prob.reshape(experts, 1, many)
 
 
@@ -272,18 +626,13 @@
     n_blk = lax.axis_size("blk")
     depth = n_blk * tokens.shape[0] // 2
     half = n_blk * CAP // 2
-    slots, probs = local_routes(expert_ids, route_probs, experts, depth)
-    all_x, all_g = (
-        lax.all_gather(
-            lax.all_gather(part, "hid", axis=1, tiled=True), "blk", axis=0, tiled=True
-        )
-        for part in (tokens, grad_out)
-    )
+    n_hid = lax.axis_size("hid")
+    all_x, all_g, ids, probs = gather_all(tokens, grad_out, expert_ids.T, route_probs.T, n_hid)
+    slots, probs = local_routes(ids, probs, experts, depth)
     dx, grad_gate, grad_up, grad_down = expert_pass(
         all_x, all_g, slots, probs, gate_w, up_w, down_w, half
     )
-    dx = lax.psum_scatter(dx, "blk", scatter_dimension=0, tiled=True)
-    grad_tokens = lax.psum_scatter(dx, "hid", scatter_dimension=1, tiled=True)
+    grad_tokens = reduce_all(dx, *tokens.shape, n_hid)
     return (grad_tokens, grad_gate, grad_up, grad_down)
 
 
@@ -291,7 +640,7 @@
     rows = n_blk * CAP
     held = 2 * (2 * 3 + 3) * width * hidden_part + (2 * 2 + 2 * 2 + 4) * many * width
     held += 4 * rows * width + 12 * rows * hidden_part
-    aligned = hidden_part % 128 == 0 and width % TILE == 0 and n_blk % 4 == 0
+    aligned = hidden_part % 128 == 0 and width % TILE == 0 and n_blk == 4
     return aligned and experts > 1 and (many // 2) % 128 == 0 and held < VMEM_ROOM
 
 

time: 309 us -> 168 us (0.54)
  waiting for transfers between devices: 193 us -> 0 us
  Pallas kernels: 86.8 us -> 161 us
  between operations: 14.1 us -> 0.68 us
  blocking collectives: 10.6 us -> 0 us
    all_gather x4 -> x0, waiting for transfers between devices: 117 us -> none  [the longest x2 60.5 us: by_tokens(): lax.all_gather(part, 'hid', axis=1, tiled=True)]
    pallas_call x0 -> x2, Pallas kernels: none -> 84.4 us  [the longest x1 53 us: gather_all(): pl.pallas_call(functools.partial(gather_kernel, n_hid), in_specs=[anywher...]
    reduce_scatter x2 -> x0, waiting for transfers between devices: 74.6 us -> none  [the longest x1 44.6 us: by_tokens(): dx = lax.psum_scatter(dx, 'blk', scatter_dimension=0, tiled=True)]
    all_gather x2 -> x0, blocking collectives: 10.6 us -> none  [the longest x1 5.32 us: local_routes(): ids = lax.all_gather(expert_ids, 'blk', axis=0, tiled=True)]
    pallas_call x1, Pallas kernels: 86.8 us -> 76.5 us  [expert_pass(): pl.pallas_call(functools.partial(expert_kernel, half), grid=(experts,), i...]
  transfers between devices with their start and end apart: 6 -> 0, of which waited for: 6 -> 0; matrix products, arithmetic and copies ran while one was open for 1% -> 0% of each run, Pallas kernels for 0% -> 0%
where the time goes in v2:
time: 168 us
  Pallas kernels  161 us (96%)
  local copies, waits for them, and re-layouts  2.93 us (2%)
  other arithmetic  2.86 us (2%)
    pallas_call x1, Pallas kernels, expert_pass(): pl.pallas_call(functools.partial(expert_kernel, half), grid=(experts,), i...  76.5 us
    pallas_call x1, Pallas kernels, gather_all(): pl.pallas_call(functools.partial(gather_kernel, n_hid), in_specs=[anywher...  53 us
    pallas_call x1, Pallas kernels, reduce_all(): pl.pallas_call(functools.partial(reduce_kernel, n_hid), in_specs=[inside]...  31.4 us

profile of v2, /device:TPU:0, one launch (start us, length us, event | category | flops | bytes accessed | tf_op | source)
XLA Modules:
  0.0 167.6 jit_solution(3005840502028616759)
XLA Ops:
  0.6 53.0 %shard_map.102 = (bf16[512,4096]{1,0:T(8,128)(2,1)}, bf16[512,4096]{1,0:T(8,128)(2,1)}, s32[32,128]{1,0:T(8,128)}, f32[32,128]{1,0:T(8,128)}) custom-call(bf16[128,1024]{1,0:T(8,128)(2,1)} %x_ref.1, bf16[128,1024]{1,0:T(8,128)(2,1)} %g_ref.1, s32[8,128]{1,0:T(8,128)} %bitcast.10, f32[8,128]{1,0:T(8,128)} %bitcast.11), custom_call_target="tpu_custom_call" | custom-call | tf_op jit(solution)/shard_map/pallas_call | solution.py:428
  53.6 0.8 compare_reduce_fusion
  54.5 1.4 fusion
  55.9 0.1 convolution_convert_fusion
  56.1 0.6 broadcast_select_fusion.slot_ref
  56.7 76.5 %shard_map.103 = (bf16[512,4096]{1,0:T(8,128)(2,1)}, bf16[4,4096,384]{2,1,0:T(8,128)(2,1)}, bf16[4,4096,384]{2,1,0:T(8,128)(2,1)}, bf16[4,384,4096]{2,1,0:T(8,128)(2,1)}) custom-call(bf16[512,4096]{1,0:T(8,128)(2,1)} %get-tuple-element.12.x_ref, bf16[512,4096]{1,0:T(8,128)(2,1)} %get-tuple-element.13.g_ref, s32[4,1,512]{2,1,0:T(1,128)} %broadcast_select_fusion.slot_ref, ...), custom_call_target="tpu_custom_call" | custom-call | flops 27380416512 | bytes 75497472 | tf_op jit(solution)/shard_map/pallas_call | solution.py:215
  133.2 0.0 copy-start
  133.2 2.2 %copy-done = bf16[512,4096]{1,0:T(8,128)(2,1)S(1)} copy-done((bf16[512,4096]{1,0:T(8,128)(2,1)S(1)}, bf16[512,4096]{1,0:T(8,128)(2,1)}, u32[]{:S(2)}) %copy-start) | copy-done | bytes 4194328
  135.4 31.4 %shard_map.104 = bf16[128,1024]{1,0:T(8,128)(2,1)S(1)} custom-call(bf16[512,4096]{1,0:T(8,128)(2,1)S(1)} %copy-done), custom_call_target="tpu_custom_call" | custom-call | tf_op jit(solution)/shard_map/pallas_call | solution.py:582
  166.9 0.7 copy.14
  (4 shorter events, 0.0 us)
Async XLA Ops:
  133.2 2.2 %copy-start = (bf16[512,4096]{1,0:T(8,128)(2,1)S(1)}, bf16[512,4096]{1,0:T(8,128)(2,1)}, u32[]{:S(2)}) copy-start(bf16[512,4096]{1,0:T(8,128)(2,1)} %get-tuple-element.16.dx_ref) | copy-start | bytes 12582916
